TPU v7x, 32 devices: a whole 2x2x4 slice. The times are simulated.
32 devices in a mesh: groups: 2 (over x), seq: 8 (over z, y), head: 2 (over core).
Axes of the slice: x: 2, y: 2, z: 4, core: 2. Of those that a mesh axis runs over, the one named last changes fastest.
Arguments:
- prompt_hidden: bfloat16 [192, 64, 7168], P(('groups', 'seq'), None, 'head'), parts along dimension 0, may hold values from -6 to 6
- prompt_len: int32 [192], P(('groups', 'seq')), parts along dimension 0, may hold values from 1 to 64
- prompt_dest: int32 [192], P(('groups', 'seq')), parts along dimension 0, may hold values from 0 to 95, as said below
- kv_weight: bfloat16 [7168, 576], P(('head', 'seq')), may hold values from -0.0625 to 0.0625
- kv_gain: float32 [512], replicated, may hold values from 0.1 to 1.9
- cache: bfloat16 [192, 256, 576], P(('groups', 'seq')), parts along dimension 0, may hold values from -4 to 4
- cache_len: int32 [192], P(('groups', 'seq')), parts along dimension 0, may hold values from 2 to 256
- step_hidden: bfloat16 [2, 192, 7168], P(None, ('groups', 'seq'), 'head'), parts along dimension 1, may hold values from -6 to 6
- queries: bfloat16 [2, 192, 128, 576], P(None, ('groups', 'seq'), 'head'), parts along dimension 1, may hold values from -300 to 300
Outputs:
- attended: bfloat16 [2, 192, 128, 512], P(None, ('groups', 'seq'), 'head'), parts along dimension 1
There are 2 independent parts, one for each index of `groups`. A program takes and returns all parts, laid end to end along the dimension named above; an argument that names none is the same for every part. Nothing has to cross between parts.
Inputs may be any that keep to these rules, and one draw needn't show every extreme that they name: `prompt_dest`: A permutation of the 96 rows; row index = device index along seq times 12 plus the row within that device. The prompts of one device go to any one device either not at all or exactly 3 at a time.
All inputs are finite; a program needn't handle non-finite values.
Results may differ from a plain program's by a relative error of at most 0.0062.
Values may be sent and summed in bfloat16 or wider, within the bound.
A program may use at most 128 MiB of HBM per device.

v0:
```python
import jax
import jax.numpy as jnp
from jax import lax
from jax.sharding import PartitionSpec as P

ROPE = 64
NOPE = 128


def normalize(projected, kv_gain):
    latent_width = kv_gain.shape[0]
    latent = projected[..., :latent_width]
    mean_square = jnp.mean(latent * latent, axis=-1, keepdims=True)
    scaled = latent * lax.rsqrt(mean_square + 1e-06) * kv_gain
    return jnp.concatenate([scaled, projected[..., latent_width:]], axis=-1).astype(jnp.bfloat16)


def attend(query_block, all_keys, visible, latent_width):
    score_scale = (NOPE + ROPE) ** (-0.5)
    scores = (
        jnp.einsum("rhc,rjc->rhj", query_block, all_keys, preferred_element_type=jnp.float32)
        * score_scale
    )
    masked = jnp.where(visible[:, None, :], scores, -jnp.inf)
    top_score = jnp.max(masked, axis=-1, keepdims=True)
    expo = jnp.exp(masked - top_score)
    weights = (expo / jnp.sum(expo, axis=-1, keepdims=True)).astype(jnp.bfloat16)
    mixed = jnp.einsum(
        "rhj,rjc->rhc", weights, all_keys[..., :latent_width], preferred_element_type=jnp.float32
    )
    return mixed.astype(jnp.bfloat16)


def on_device(
    prompt_hidden,
    prompt_len,
    prompt_dest,
    kv_weight,
    kv_gain,
    cache,
    cache_len,
    step_hidden,
    queries,
):
    rows_here, prompt_slots, half_model = prompt_hidden.shape
    step_count = step_hidden.shape[0]
    cache_width = kv_weight.shape[1]
    resident_slots = cache.shape[1]
    latent_width = kv_gain.shape[0]
    devices = lax.axis_size("seq")
    capacity = max(1, 2 * rows_here // devices)
    prompt_rows = prompt_hidden.reshape(rows_here * prompt_slots, half_model)
    step_rows = step_hidden.reshape(step_count * rows_here, half_model)
    weight_piece = lax.all_gather(kv_weight, "seq", axis=0, tiled=True)
    prompt_part = jnp.dot(prompt_rows, weight_piece, preferred_element_type=jnp.float32)
    step_part = jnp.dot(step_rows, weight_piece, preferred_element_type=jnp.float32)
    prompt_sum, step_sum = lax.psum((prompt_part, step_part), "head")
    prompt_sum = prompt_sum.reshape(rows_here, prompt_slots, cache_width)
    pages = normalize(prompt_sum, kv_gain)
    fresh = normalize(step_sum, kv_gain).reshape(step_count, rows_here, cache_width)
    target = prompt_dest // rows_here
    earlier = jnp.arange(rows_here)[None, :] < jnp.arange(rows_here)[:, None]
    same_target = target[None, :] == target[:, None]
    order_index = jnp.sum((earlier & same_target).astype(jnp.int32), axis=1)
    send_slot = target * capacity + order_index
    outgoing = (
        jnp.zeros((devices * capacity,) + pages.shape[1:], jnp.bfloat16).at[send_slot].set(pages)
    )
    labels = jnp.full((devices * capacity, 2), -1, jnp.int32)
    labels = labels.at[send_slot].set(jnp.stack([prompt_dest % rows_here, prompt_len], axis=1))
    incoming, metadata = (
        lax.all_to_all(outgoing, "seq", split_axis=0, concat_axis=0, tiled=True),
        lax.all_to_all(labels, "seq", split_axis=0, concat_axis=0, tiled=True),
    )
    row_match = metadata[:, 0][None, :] == jnp.arange(rows_here)[:, None]
    slot_index = jnp.arange(devices * capacity, dtype=jnp.int32)[None, :]
    source_slot = jnp.sum(jnp.where(row_match, slot_index, 0), axis=1)
    arrived = incoming[source_slot]
    arrived_len = metadata[source_slot, 1]
    all_keys = jnp.concatenate([cache, arrived, jnp.transpose(fresh, (1, 0, 2))], axis=1)
    position = jnp.arange(resident_slots + prompt_slots + step_count, dtype=jnp.int32)[None, :]
    resident = position < cache_len[:, None]
    prompt_part_mask = (position >= resident_slots) & (
        position < resident_slots + arrived_len[:, None]
    )
    outputs = []
    for step_index in range(step_count):
        fresh_part = (position >= resident_slots + prompt_slots) & (
            position <= resident_slots + prompt_slots + step_index
        )
        visible = resident | prompt_part_mask | fresh_part
        outputs.append(attend(queries[step_index], all_keys, visible, latent_width))
    return jnp.stack(outputs)


def solution(mesh):
    in_specs = (
        P(("groups", "seq"), None, "head"),
        P(("groups", "seq")),
        P(("groups", "seq")),
        P(("head", "seq"), None),
        P(),
        P(("groups", "seq"), None, None),
        P(("groups", "seq")),
        P(None, ("groups", "seq"), "head"),
        P(None, ("groups", "seq"), "head", None),
    )
    out_specs = P(None, ("groups", "seq"), "head", None)
    return jax.shard_map(
        on_device, mesh=mesh, in_specs=in_specs, out_specs=out_specs, check_vma=False
    )
```

profile of v0, /device:TPU:29, one launch (start us, length us, event | category | flops | bytes accessed | tf_op | source)
XLA Modules:
  0.0 202.3 jit_solution(11919864941559395331)
XLA Ops:
  6.5 0.7 all-gather.2.cloned.1.call-update
  7.3 78.8 %all-gather.2.cloned.1.call-done = bf16[3584,576]{1,0:T(8,128)(2,1)} async-done(((bf16[448,576]{1,0:T(8,128)(2,1)}), bf16[3584,576]{1,0:T(8,128)(2,1)}) %all-gather.2.cloned.1.call-update) | async-done | bytes 4128784 | tf_op jit(solution)/shard_map/all_gather | solution.py:54
  86.1 9.7 %fusion.41 = f32[768,576]{1,0:T(8,128)} fusion(bf16[768,3584]{1,0:T(8,128)(2,1)} %bitcast.49, bf16[3584,576]{1,0:T(8,128)(2,1)} %all-gather.2.cloned.1.call-done), kind=kOutput, calls=%fused_computation.81 | convolution fusion | flops 3170893824 | bytes 11403264 | tf_op jit(solution)/shard_map/dot_general | solution.py:55
  95.8 0.6 copy-done.5
  96.8 0.6 scatter_custom_fusion
  97.6 0.6 copy.31
  98.2 5.5 %all-to-all-start = ((s32[8,3,2]{1,2,0:T(2,128)}), s32[8,3,2]{1,2,0:T(2,128)S(1)}, u32[]{:S(2)}, u32[]{:S(2)}) async-start(s32[8,3,2]{1,2,0:T(2,128)} %copy.31), calls=%async_computation | async-start | bytes 16384 | tf_op jit(solution)/shard_map/all_to_all | solution.py:73
  103.7 14.9 %all-reduce.3.cloned.1.call-done = f32[12,64,576]{2,1,0:T(8,128)} async-done(((f32[12,64,576]{2,1,0:T(8,128)}), f32[12,64,576]{2,1,0:T(8,128)}) %all-reduce.3.cloned.1.call-update) | async-done | bytes 1769488 | tf_op jit(solution)/shard_map/psum | solution.py:57
  118.6 1.7 multiply_reduce_fusion
  120.3 1.0 slice.58
  121.7 1.6 broadcast_in_dim.66
  123.3 3.0 %scatter_fusion = bf16[24,64,576]{2,1,0:T(8,128)(2,1)} fusion(bf16[24,64,576]{2,1,0:T(8,128)(2,1)} %broadcast_in_dim.66, s32[12]{0:T(128)S(1)} %compare_select_fusion.1, bf16[12,64,576]{2,1,0:T(8,128)(2,1)S(1)} %pad_maximum_fusion.19), kind=kCustom, calls=%fused_computation.3 | custom fusion | bytes 2654256 | tf_op jit(solution)/shard_map/scatter | solution.py:67
  126.3 5.6 %all-to-all-start.1 = ((bf16[24,64,576]{2,1,0:T(8,128)(2,1)}), bf16[24,64,576]{2,1,0:T(8,128)(2,1)S(1)}, u32[]{:S(2)}, u32[]{:S(2)}) async-start(bf16[24,64,576]{2,1,0:T(8,128)(2,1)} %scatter_fusion), calls=%async_computation.1 | async-start | bytes 3932160 | tf_op jit(solution)/shard_map/all_to_all | solution.py:72
  132.0 6.0 %copy.37 = bf16[12,256,576]{2,1,0:T(8,128)(2,1)} copy(bf16[12,256,576]{1,2,0:T(8,128)(2,1)} %param.14) | data formatting | bytes 7077888 | tf_op args[5]
  138.2 0.7 gather_fusion
  139.1 3.0 %fusion.42 = f32[24,576]{1,0:T(8,128)S(1)} fusion(bf16[24,3584]{1,0:T(8,128)(2,1)S(1)} %reshape.193, bf16[3584,576]{1,0:T(8,128)(2,1)} %all-gather.2.cloned.1.call-done), kind=kOutput, calls=%fused_computation.82 | convolution fusion | flops 99090432 | bytes 4356096 | tf_op jit(solution)/shard_map/dot_general | solution.py:56
  142.1 4.2 %psum.15 = f32[24,576]{1,0:T(8,128)S(1)} all-reduce(f32[24,576]{1,0:T(8,128)S(1)} %fusion.42), channel_id=1, replica_groups=mesh['groups'=2,'seq'=8,'head'=2] {'head'}, use_global_device_ids=true, to_apply=%region_6.7 | all-reduce | flops 13824 | bytes 110592 | tf_op jit(solution)/shard_map/psum | solution.py:57
  146.6 29.1 %all-to-all-done.1 = bf16[24,64,576]{2,1,0:T(8,128)(2,1)S(1)} async-done(((bf16[24,64,576]{2,1,0:T(8,128)(2,1)}), bf16[24,64,576]{2,1,0:T(8,128)(2,1)S(1)}, u32[]{:S(2)}, u32[]{:S(2)}) %all-to-all-start.1) | async-done | bytes 1769504 | tf_op jit(solution)/shard_map/all_to_all | solution.py:72
  175.7 0.7 gather_fusion.1
  176.4 4.0 %fusion.13 = f32[12,64,322]{2,1,0:T(8,128)S(1)} fusion(bf16[12,2,576]{2,1,0:T(2,128)(2,1)S(1)} %maximum_bitcast_fusion, bf16[12,64,576]{2,1,0:T(8,128)(2,1)S(1)} %gather_fusion.1, bf16[12,256,576]{2,1,0:T(8,128)(2,1)} %copy.37, bf16[2,12,64,576]{3,2,1,0:T(8,128)(2,1)} %param.17, pred[12,322]{1,0:T(8,128)(4,1)S(1)} %get-tuple-element.6), kind=kOutput, calls=%fused_computation.24 | convolution fusion | flops 298733568 | bytes 6820632 | tf_op jit(solution)/shard_map/rhc,rjc->rhj/dot_general | solution.py:21
  180.8 3.5 %fusion.11 = bf16[1,12,64,512]{3,2,1,0:T(8,128)(2,1)S(1)} fusion(bf16[12,2,576]{2,1,0:T(2,128)(2,1)S(1)} %maximum_bitcast_fusion, bf16[12,64,576]{2,1,0:T(8,128)(2,1)S(1)} %gather_fusion.1, bf16[12,256,576]{2,1,0:T(8,128)(2,1)} %copy.37, f32[12,64]{1,0:T(8,128)S(1)} %fusion.39, f32[12,64,322]{2,1,0:T(8,128)S(1)} %fusion.13), kind=kOutput, calls=%fused_computation.22 | convolution fusion | flops 266237504 | bytes 6230016 | tf_op jit(solution)/shard_map/rhj,rjc->rhc/dot_general | solution.py:28
  184.3 4.0 %fusion.15 = f32[12,64,322]{2,1,0:T(8,128)S(1)} fusion(bf16[12,2,576]{2,1,0:T(2,128)(2,1)S(1)} %maximum_bitcast_fusion, bf16[12,64,576]{2,1,0:T(8,128)(2,1)S(1)} %gather_fusion.1, bf16[12,256,576]{2,1,0:T(8,128)(2,1)} %copy.37, bf16[2,12,64,576]{3,2,1,0:T(8,128)(2,1)} %param.17, pred[12,322]{1,0:T(8,128)(4,1)S(1)} %get-tuple-element.5), kind=kOutput, calls=%fused_computation.26 | convolution fusion | flops 298733568 | bytes 6820632 | tf_op jit(solution)/shard_map/rhc,rjc->rhj/dot_general | solution.py:21
  188.7 4.4 %fusion.10 = bf16[1,12,64,512]{3,2,1,0:T(8,128)(2,1)} fusion(bf16[12,2,576]{2,1,0:T(2,128)(2,1)S(1)} %maximum_bitcast_fusion, bf16[12,64,576]{2,1,0:T(8,128)(2,1)S(1)} %gather_fusion.1, bf16[12,256,576]{2,1,0:T(8,128)(2,1)} %copy.37, f32[12,64]{1,0:T(8,128)S(1)} %fusion.40, f32[12,64,322]{2,1,0:T(8,128)S(1)} %fusion.15), kind=kOutput, calls=%fused_computation.21 | convolution fusion | flops 266237504 | bytes 6230016 | tf_op jit(solution)/shard_map/rhj,rjc->rhc/dot_general | solution.py:28
  193.0 2.4 %pad_maximum_fusion.4 = bf16[2,12,64,512]{3,2,1,0:T(8,128)(2,1)} fusion(bf16[1,12,64,512]{3,2,1,0:T(8,128)(2,1)S(1)} %fusion.11, bf16[1,12,64,512]{3,2,1,0:T(8,128)(2,1)} %fusion.10), kind=kLoop, calls=%fused_computation.10 | loop fusion | flops 786432 | bytes 3145728 | tf_op jit(solution)/shard_map/stack | solution.py:93
  (48 shorter events, 2.2 us)
Async XLA Ops:
  6.5 79.6 %all-gather.2.cloned.1.call-start = ((), (), s32[]{:S(2)}) async-start(), calls=%async_computation.2 | async-start | bytes 5160960 | tf_op jit(solution)/shard_map/all_gather | solution.py:54
  7.3 111.3 %all-reduce.3.cloned.1.call-start = ((), (), s32[]{:S(2)}) async-start(), calls=%async_computation.3 | async-start | bytes 3932160 | tf_op jit(solution)/shard_map/psum | solution.py:57
  95.8 0.7 copy-start.5
  95.8 0.7 copy-start.3
  95.8 25.6 %copy-start.2 = (f32[512]{0:T(512)S(1)}, f32[512]{0:T(512)}, u32[]{:S(2)}) copy-start(f32[512]{0:T(512)} %param.13) | copy-start | bytes 6148
  98.2 28.2 %all-to-all-start = ((s32[8,3,2]{1,2,0:T(2,128)}), s32[8,3,2]{1,2,0:T(2,128)S(1)}, u32[]{:S(2)}, u32[]{:S(2)}) async-start(s32[8,3,2]{1,2,0:T(2,128)} %copy.31), calls=%async_computation | async-start | bytes 16384 | tf_op jit(solution)/shard_map/all_to_all | solution.py:73
  118.6 2.8 %copy-start = (f32[12,64,576]{2,1,0:T(8,128)S(1)}, f32[12,64,576]{2,1,0:T(8,128)}, u32[]{:S(2)}) copy-start(f32[12,64,576]{2,1,0:T(8,128)} %all-reduce.3.cloned.1.call-done) | copy-start | bytes 5308420
  126.3 5.6 %copy-start.1 = (bf16[2,12,3584]{2,0,1:T(2,128)(2,1)S(1)}, bf16[2,12,3584]{2,0,1:T(2,128)(2,1)}, u32[]{:S(2)}) copy-start(bf16[2,12,3584]{2,0,1:T(2,128)(2,1)} %param.16) | copy-start | bytes 516100
  126.3 49.4 %all-to-all-start.1 = ((bf16[24,64,576]{2,1,0:T(8,128)(2,1)}), bf16[24,64,576]{2,1,0:T(8,128)(2,1)S(1)}, u32[]{:S(2)}, u32[]{:S(2)}) async-start(bf16[24,64,576]{2,1,0:T(8,128)(2,1)} %scatter_fusion), calls=%async_computation.1 | async-start | bytes 3932160 | tf_op jit(solution)/shard_map/all_to_all | solution.py:72
  132.0 7.0 %copy-start.4 = (s32[12]{0:T(128)S(1)}, s32[12]{0:T(128)}, u32[]{:S(2)}) copy-start(s32[12]{0:T(128)} %param.15) | copy-start | bytes 148
Sparse Core Ops, SparseCore 0:
  9.5 76.5 all-gather.1
  95.9 22.5 all-reduce.2
where the time goes:
time: 206 us; the launch traced here: 202 us
  waiting for transfers between devices  124 us (60%)
  matrix products  28.5 us (14%)
  local copies, waits for them, and re-layouts  15.4 us (7%)
  between operations  13.6 us (7%)
  starting transfers between devices  11.1 us (5%)
  other arithmetic  5.84 us (3%)
  blocking collectives  4.18 us (2%)
    all_gather x1, waiting for transfers between devices, on_device(): weight_piece = lax.all_gather(kv_weight, 'seq', axis=0, tiled=True)  78.8 us
    all_to_all x1, waiting for transfers between devices, on_device(): lax.all_to_all(outgoing, 'seq', split_axis=0, concat_axis=0, tiled=True)  29.1 us
    psum x1, waiting for transfers between devices, on_device(): prompt_sum, step_sum = lax.psum((prompt_part, step_part), 'head')  14.9 us
    dot_general x1, matrix products, on_device(): jnp.dot(prompt_rows, weight_piece, preferred_element_type=jnp.float32)  9.66 us
    dot_general x2, matrix products, attend(): jnp.einsum('rhc,rjc->rhj', query_block, all_keys, preferred_element_type=...  7.98 us
    dot_general x2, matrix products, attend(): jnp.einsum('rhj,rjc->rhc', weights, all_keys[..., :latent_width], preferr...  7.86 us
    unnamed x14, local copies, waits for them, and re-layouts  6.64 us
    all_to_all x1, starting transfers between devices, on_device(): lax.all_to_all(outgoing, 'seq', split_axis=0, concat_axis=0, tiled=True)  5.57 us
  transfers between devices with their start and end apart: 4, of which 3 were waited for; matrix products, arithmetic and copies ran while one was open for 10% of the time, Pallas kernels for 0%

commit v1 on v0

v1 whole, which is shorter than its diff:
```python
import functools

import jax
import jax.numpy as jnp
from jax import lax
from jax.experimental import pallas as pl
from jax.experimental.pallas import tpu as pltpu
from jax.sharding import PartitionSpec as P

ROPE = 64
NOPE = 128
BLOCKS = 4
TILE = 16
MESH = pl.DeviceIdType.MESH


def ring_place(index, n, snake):
    if not snake:
        return index
    plane, column = lax.div(index, 2), lax.rem(index, 2)
    return plane + column * (n - 1 - 2 * plane)


def ring_index(place, n, snake):
    place = lax.rem(place + n, n)
    if not snake:
        return place
    back = lax.div(place, n // 2)
    return (1 - back) * 2 * place + back * (2 * (n - 1 - place) + 1)


def project_kernel(
    n,
    cap,
    snake,
    send_prompt,
    hidden,
    step_rows,
    weight,
    gain,
    labels,
    inbox,
    meta,
    fresh,
    hbuf,
    wall,
    acc,
    other,
    pages,
    outbox,
    local_sem,
    ring_send,
    ring_recv,
    cross_send,
    cross_recv,
    pair_send,
    pair_recv,
    page_send,
    page_recv,
    mate_send,
    mate_recv,
    meta_send,
    meta_recv,
):
    rows, tokens, depth = hidden.shape
    half = tokens // 2
    shard, width = weight.shape
    latent_width = gain.shape[1]
    near = ((shard + TILE - 1) // (3 * TILE)) * TILE
    far = shard - near
    steps = n // 2

    group = lax.axis_index("groups")
    me = lax.axis_index("seq")
    core = lax.axis_index("head")
    side = lax.rem(group, 2)
    twin = {"groups": group + 1 - 2 * side, "seq": me, "head": core}
    mate = {"groups": group, "seq": me, "head": 1 - core}

    def peer(index):
        return {"groups": group, "seq": index, "head": core}

    place = ring_place(me, n, snake)

    own = pltpu.make_async_copy(weight, wall.at[me], local_sem.at[0])
    own.start()
    loads = [
        pltpu.make_async_copy(
            hidden.at[:, pl.ds(pl.multiple_of((1 - core) * half, half), half), :],
            hbuf.at[pl.ds(0, rows)],
            local_sem.at[1],
        ),
        pltpu.make_async_copy(step_rows, hbuf.at[rows], local_sem.at[2]),
        pltpu.make_async_copy(
            hidden.at[:, pl.ds(pl.multiple_of(core * half, half), half), :],
            hbuf.at[pl.ds(rows + 1, rows)],
            local_sem.at[3],
        ),
    ]

    barrier = pltpu.get_barrier_semaphore()
    for offset in range(1, n):
        pl.semaphore_signal(
            barrier, inc=1, device_id=peer(lax.rem(me + offset, n)), device_id_type=MESH
        )
    pl.semaphore_signal(barrier, inc=1, device_id=twin, device_id_type=MESH)
    pl.semaphore_signal(barrier, inc=1, device_id=mate, device_id_type=MESH)
    pl.semaphore_wait(barrier, n + 1)
    own.wait()

    def span(chunk, which):
        if chunk == 0:
            return pl.ds(pl.multiple_of(which * far, TILE), near)
        return pl.ds(near, far - near)

    def ring_copy(way, step, chunk):
        sign = 1 - 2 * way
        block = wall.at[ring_index(place - sign * (step - 1), n, snake), span(chunk, side)]
        return pltpu.make_async_remote_copy(
            src_ref=block,
            dst_ref=block,
            send_sem=ring_send.at[way, step - 1, chunk],
            recv_sem=ring_recv.at[way, step - 1, chunk],
            device_id=peer(ring_index(place + sign, n, snake)),
            device_id_type=MESH,
        )

    def ring_arrival(way, step, chunk):
        sign = 1 - 2 * way
        block = wall.at[ring_index(place - sign * step, n, snake), span(chunk, side)]
        return pltpu.make_async_remote_copy(
            src_ref=block,
            dst_ref=block,
            send_sem=ring_send.at[way, step - 1, chunk],
            recv_sem=ring_recv.at[way, step - 1, chunk],
            device_id=peer(ring_index(place + sign, n, snake)),
            device_id_type=MESH,
        )

    def cross_copy(way, step, which):
        sign = 1 - 2 * way
        block = wall.at[ring_index(place - sign * step, n, snake), span(0, which)]
        return pltpu.make_async_remote_copy(
            src_ref=block,
            dst_ref=block,
            send_sem=cross_send.at[way, step - 1],
            recv_sem=cross_recv.at[way, step - 1],
            device_id=twin,
            device_id_type=MESH,
        )

    def goes(way, step, chunk):
        return step < steps or (step == steps and way == chunk)

    for chunk in (0, 1):
        for way in (0, 1):
            if goes(way, 1, chunk):
                ring_copy(way, 1, chunk).start()
    for load in loads:
        load.start()

    def meta_copy(target, row):
        return pltpu.make_async_remote_copy(
            src_ref=labels.at[target],
            dst_ref=meta.at[row],
            send_sem=meta_send.at[target],
            recv_sem=meta_recv.at[row],
            device_id=peer(target),
            device_id_type=MESH,
        )

    for offset in range(1, n):
        meta_copy(lax.rem(me + offset, n), me).start()
    own_meta = pltpu.make_async_copy(labels.at[me], meta.at[me], local_sem.at[0])
    own_meta.start()
    for load in loads:
        load.wait()

    depth_block = depth // BLOCKS
    shards_block = n // BLOCKS
    lower = pl.ds(0, rows + 1)
    upper = pl.ds(rows + 1, rows)

    def block_at(turn):
        if not snake:
            return jnp.int32(turn)
        plane = lax.div(me, 2)
        late = lax.div(plane, BLOCKS // 2)
        edge = plane + late * (BLOCKS - 1 - 2 * plane)
        base = (jnp.int32(0), jnp.int32(1), 2 + edge, 3 - edge)[turn]
        return base + late * (BLOCKS - 1 - 2 * base)

    def multiply(turn, part, count):
        block = block_at(turn)
        columns = pl.ds(pl.multiple_of(block * depth_block, 128), depth_block)
        left = hbuf[part, :, columns].reshape(count * half, depth_block)
        right = wall[pl.ds(block * shards_block, shards_block)].reshape(depth_block, width)
        product = jnp.dot(left, right, preferred_element_type=jnp.float32)
        product = product.reshape(count, half, width)
        if turn == 0:
            acc[part] = product
        else:
            acc[part] += product

    ready = {2: (0,), 3: (1, 2), 4: (3,)} if snake else {steps: tuple(range(BLOCKS))}
    crossed = []
    for step in range(1, steps + 1):
        for chunk in (0, 1):
            for way in (0, 1):
                if not goes(way, step, chunk):
                    continue
                ring_arrival(way, step, chunk).wait_recv()
                if step < steps and goes(way, step + 1, chunk):
                    ring_copy(way, step + 1, chunk).start()
                if chunk == 0:
                    cross_copy(way, step, side).start()
                    crossed.append((way, step))
        turns = ready.get(step, ())
        if turns:
            for way, when in crossed:
                cross_copy(way, when, 1 - side).wait_recv()
            crossed = []
        for turn in turns:
            multiply(turn, lower, rows + 1)
            if turn == BLOCKS - 1:
                pair = pltpu.make_async_remote_copy(
                    src_ref=acc.at[lower],
                    dst_ref=other,
                    send_sem=pair_send,
                    recv_sem=pair_recv,
                    device_id=mate,
                    device_id_type=MESH,
                )
                pair.start()
            multiply(turn, upper, rows)
    pair.wait()

    scale = gain[...]

    def norm(value):
        latent = value[:, :latent_width]
        mean_square = jnp.mean(latent * latent, axis=-1, keepdims=True)
        return latent * lax.rsqrt(mean_square + 1e-06) * scale, value[:, latent_width:]

    def norm_page(row, carry):
        value = acc[rows + 1 + row] + other[row]
        head_part, tail_part = norm(value)
        pages[row, :, :latent_width] = head_part.astype(jnp.bfloat16)
        pages[row, :, latent_width:] = tail_part.astype(jnp.bfloat16)
        return carry

    lax.fori_loop(0, rows, norm_page, 0)

    def page_copy(target, row):
        return pltpu.make_async_remote_copy(
            src_ref=outbox.at[target],
            dst_ref=inbox.at[core, row],
            send_sem=page_send.at[target],
            recv_sem=page_recv.at[row],
            device_id=peer(target),
            device_id_type=MESH,
        )

    def mate_copy(row, from_outbox, where):
        return pltpu.make_async_remote_copy(
            src_ref=outbox.at[row] if from_outbox else inbox.at[where, row],
            dst_ref=inbox.at[where, row],
            send_sem=mate_send.at[row],
            recv_sem=mate_recv.at[row],
            device_id=mate,
            device_id_type=MESH,
        )

    for offset in list(range(1, n)) + [0]:
        target = lax.rem(me + offset, n)
        for slot in range(cap):
            outbox[target, pl.ds(slot * half, half), :] = pages[send_prompt[target * cap + slot]]
        if offset:
            page_copy(target, me).start()
    own_meta.wait()
    own_page = pltpu.make_async_copy(outbox.at[me], inbox.at[core, me], local_sem.at[0])
    own_page.start()
    mate_copy(me, True, core).start()

    head_part, tail_part = norm(acc[rows] + other[rows])
    fresh[:, :latent_width] = head_part.astype(jnp.bfloat16).astype(jnp.float32)
    fresh[:, latent_width:] = tail_part.astype(jnp.bfloat16).astype(jnp.float32)

    for step in range(1, steps + 1):
        for chunk in (0, 1):
            for way in (0, 1):
                if goes(way, step, chunk):
                    ring_copy(way, step, chunk).wait_send()
                    if chunk == 0:
                        cross_copy(way, step, side).wait_send()
    for offset in range(1, n):
        source = lax.rem(me + n - offset, n)
        page_copy(source, source).wait_recv()
        mate_copy(source, False, core).start()
    for offset in range(1, n):
        target = lax.rem(me + offset, n)
        page_copy(target, me).wait_send()
        meta_copy(target, me).wait_send()
        meta_copy(target, target).wait_recv()
    own_page.wait()
    for offset in range(n):
        source = lax.rem(me + n - offset, n)
        mate_copy(source, offset == 0, 1 - core).wait_recv()
        mate_copy(source, offset == 0, core).wait_send()


def attend_kernel(
    rows, slot_of, arrived_len, cache_len, query, cache, page, fresh, out, recent
):
    row = pl.program_id(0)
    step_count, _, heads, width = query.shape
    latent_width = out.shape[-1]
    half = page.shape[2]
    tokens = 2 * half
    recent[pl.ds(0, tokens), :] = page[...].reshape(tokens, width)
    spot = lax.broadcasted_iota(jnp.int32, (TILE, width), 0)
    tail = jnp.zeros((TILE, width), jnp.float32)
    for step in range(step_count):
        tail = jnp.where(spot == step, fresh[pl.ds(step * rows + row, 1), :], tail)
    recent[pl.ds(tokens, TILE), :] = tail.astype(jnp.bfloat16)

    score_scale = (NOPE + ROPE) ** (-0.5)
    asked = query[...].reshape(step_count * heads, width)
    resident_keys = cache[0]
    recent_keys = recent[...]
    contract = (((1,), (1,)), ((), ()))
    old = lax.dot_general(asked, resident_keys, contract, preferred_element_type=jnp.float32)
    new = lax.dot_general(asked, recent_keys, contract, preferred_element_type=jnp.float32)
    old_spot = lax.broadcasted_iota(jnp.int32, old.shape, 1)
    new_spot = lax.broadcasted_iota(jnp.int32, new.shape, 1)
    step_of = lax.div(lax.broadcasted_iota(jnp.int32, new.shape, 0), heads)
    old = jnp.where(old_spot < cache_len[row], old * score_scale, -jnp.inf)
    seen = (new_spot < arrived_len[row]) | (
        (new_spot >= tokens) & (new_spot <= tokens + step_of)
    )
    new = jnp.where(seen, new * score_scale, -jnp.inf)
    top = jnp.maximum(
        jnp.max(old, axis=-1, keepdims=True), jnp.max(new, axis=-1, keepdims=True)
    )
    old = jnp.exp(old - top)
    new = jnp.exp(new - top)
    inverse = 1.0 / (
        jnp.sum(old, axis=-1, keepdims=True) + jnp.sum(new, axis=-1, keepdims=True)
    )
    mixed = jnp.dot(
        (old * inverse).astype(jnp.bfloat16),
        resident_keys[:, :latent_width],
        preferred_element_type=jnp.float32,
    ) + jnp.dot(
        (new * inverse).astype(jnp.bfloat16),
        recent_keys[:, :latent_width],
        preferred_element_type=jnp.float32,
    )
    out[...] = mixed.astype(jnp.bfloat16).reshape(out.shape)


def on_device(
    snake,
    prompt_hidden,
    prompt_len,
    prompt_dest,
    kv_weight,
    kv_gain,
    cache,
    cache_len,
    step_hidden,
    queries,
):
    rows, tokens, depth = prompt_hidden.shape
    step_count = step_hidden.shape[0]
    shard, width = kv_weight.shape
    resident_slots = cache.shape[1]
    latent_width = kv_gain.shape[0]
    heads = queries.shape[2]
    n = lax.axis_size("seq")
    cap = max(1, 2 * rows // n)
    half = tokens // 2

    step_rows = step_hidden.reshape(step_count * rows, depth)
    step_rows = jnp.pad(step_rows, ((0, half - step_count * rows), (0, 0)))

    target = prompt_dest // rows
    ids = jnp.arange(rows, dtype=jnp.int32)
    earlier = (ids[None, :] < ids[:, None]) & (target[None, :] == target[:, None])
    send_slot = target * cap + jnp.sum(earlier.astype(jnp.int32), axis=1)
    slots = jnp.arange(n * cap, dtype=jnp.int32)
    fits = send_slot[None, :] == slots[:, None]
    send_prompt = jnp.sum(jnp.where(fits, ids[None, :], 0), axis=1)
    label_row = jnp.sum(jnp.where(fits, prompt_dest[None, :] % rows + 1, 0), axis=1) - 1
    label_len = jnp.sum(jnp.where(fits, prompt_len[None, :], 0), axis=1)
    labels = jnp.stack([label_row.reshape(n, cap), label_len.reshape(n, cap)], axis=1)
    labels = jnp.pad(labels, ((0, 0), (0, 6), (0, 128 - cap)))

    dma = pltpu.SemaphoreType.DMA
    anywhere = pl.BlockSpec(memory_space=pl.ANY)
    in_vmem = pl.BlockSpec(memory_space=pltpu.VMEM)
    inbox, meta, fresh = pl.pallas_call(
        functools.partial(project_kernel, n, cap, snake),
        out_shape=(
            jax.ShapeDtypeStruct((2, n, cap * half, width), jnp.bfloat16),
            jax.ShapeDtypeStruct((n, 8, 128), jnp.int32),
            jax.ShapeDtypeStruct((half, width), jnp.float32),
        ),
        in_specs=[
            pl.BlockSpec(memory_space=pltpu.SMEM),
            anywhere,
            anywhere,
            anywhere,
            in_vmem,
            anywhere,
        ],
        out_specs=(anywhere, anywhere, in_vmem),
        scratch_shapes=[
            pltpu.VMEM((2 * rows + 1, half, depth), jnp.bfloat16),
            pltpu.VMEM((n, shard, width), jnp.bfloat16),
            pltpu.VMEM((2 * rows + 1, half, width), jnp.float32),
            pltpu.VMEM((rows + 1, half, width), jnp.float32),
            pltpu.VMEM((rows, half, width), jnp.bfloat16),
            pltpu.VMEM((n, cap * half, width), jnp.bfloat16),
            dma((4,)),
            dma((2, n // 2, 2)),
            dma((2, n // 2, 2)),
            dma((2, n // 2)),
            dma((2, n // 2)),
            dma,
            dma,
            dma((n,)),
            dma((n,)),
            dma((n,)),
            dma((n,)),
            dma((n,)),
            dma((n,)),
        ],
        compiler_params=pltpu.CompilerParams(
            collective_id=0, has_side_effects=True, vmem_limit_bytes=48 * 1024 * 1024
        ),
    )(
        send_prompt,
        prompt_hidden,
        step_rows,
        kv_weight,
        kv_gain.reshape(1, latent_width),
        labels,
    )

    came_row = meta[:, 0, :cap].reshape(-1)
    came_len = meta[:, 1, :cap].reshape(-1)
    match = came_row[None, :] == ids[:, None]
    slot_of = jnp.sum(jnp.where(match, slots[None, :], 0), axis=1)
    arrived_len = jnp.sum(jnp.where(match, came_len[None, :], 0), axis=1)

    return pl.pallas_call(
        functools.partial(attend_kernel, rows),
        grid_spec=pltpu.PrefetchScalarGridSpec(
            num_scalar_prefetch=3,
            grid=(rows,),
            in_specs=[
                pl.BlockSpec((step_count, 1, heads, width), lambda r, *_: (0, r, 0, 0)),
                pl.BlockSpec((1, resident_slots, width), lambda r, *_: (r, 0, 0)),
                pl.BlockSpec((2, 1, half, width), lambda r, slot, *_: (0, slot[r], 0, 0)),
                pl.BlockSpec((half, width), lambda r, *_: (0, 0)),
            ],
            out_specs=pl.BlockSpec(
                (step_count, 1, heads, latent_width), lambda r, *_: (0, r, 0, 0)
            ),
            scratch_shapes=[pltpu.VMEM((tokens + TILE, width), jnp.bfloat16)],
        ),
        out_shape=jax.ShapeDtypeStruct((step_count, rows, heads, latent_width), jnp.bfloat16),
        compiler_params=pltpu.CompilerParams(vmem_limit_bytes=32 * 1024 * 1024),
    )(
        slot_of,
        arrived_len,
        cache_len,
        queries,
        cache,
        inbox.reshape(2, n * cap, half, width),
        fresh,
    )


def solution(mesh):
    snake = mesh.shape["seq"] == 2 * BLOCKS
    in_specs = (
        P(("groups", "seq"), None, "head"),
        P(("groups", "seq")),
        P(("groups", "seq")),
        P(("head", "seq"), None),
        P(),
        P(("groups", "seq"), None, None),
        P(("groups", "seq")),
        P(None, ("groups", "seq"), "head"),
        P(None, ("groups", "seq"), "head", None),
    )
    out_specs = P(None, ("groups", "seq"), "head", None)
    return jax.shard_map(
        functools.partial(on_device, snake),
        mesh=mesh,
        in_specs=in_specs,
        out_specs=out_specs,
        check_vma=False,
    )
```

time: 206 us -> 101 us (0.49); the launches traced: 202 us -> 100 us
  waiting for transfers between devices: 124 us -> 0 us
  Pallas kernels: 0 us -> 84.4 us
  matrix products: 28.5 us -> 0 us
  between operations: 13.6 us -> 0.1 us
  starting transfers between devices: 11.1 us -> 0 us
  blocking collectives: 4.18 us -> 0 us
  other arithmetic: 5.84 us -> 1.74 us
    pallas_call x0 -> x2, Pallas kernels: none -> 84.4 us  [the longest x1 73.5 us: on_device(): pl.pallas_call(functools.partial(project_kernel, n, cap, snake), out_shap...]
    all_gather x1 -> x0, waiting for transfers between devices: 78.8 us -> none  [on_device(): weight_piece = lax.all_gather(kv_weight, 'seq', axis=0, tiled=True)]
    all_to_all x2 -> x0, waiting for transfers between devices: 29.1 us -> none  [the longest x1 29.1 us: on_device(): lax.all_to_all(outgoing, 'seq', split_axis=0, concat_axis=0, tiled=True)]
    dot_general x6 -> x0, matrix products: 28.5 us -> none  [the longest x1 9.66 us: on_device(): jnp.dot(prompt_rows, weight_piece, preferred_element_type=jnp.float32)]
    psum x1 -> x0, waiting for transfers between devices: 14.9 us -> none  [on_device(): prompt_sum, step_sum = lax.psum((prompt_part, step_part), 'head')]
    all_to_all x2 -> x0, starting transfers between devices: 11.1 us -> none  [the longest x1 5.57 us: on_device(): lax.all_to_all(outgoing, 'seq', split_axis=0, concat_axis=0, tiled=True)]
    unnamed x14 -> x16, local copies, waits for them, and re-layouts: 6.64 us -> 13.7 us
    psum x1 -> x0, blocking collectives: 4.18 us -> none  [on_device(): prompt_sum, step_sum = lax.psum((prompt_part, step_part), 'head')]
  transfers between devices with their start and end apart: 4 -> 0, of which waited for: 3 -> 0; matrix products, arithmetic and copies ran while one was open for 10% -> 0% of each run, Pallas kernels for 0% -> 0%
where the time goes in v1:
time: 101 us; the launch traced here: 100 us
  Pallas kernels  84.4 us (84%)
  local copies, waits for them, and re-layouts  14.1 us (14%)
  other arithmetic  1.74 us (2%)
    pallas_call x1, Pallas kernels, on_device(): pl.pallas_call(functools.partial(project_kernel, n, cap, snake), out_shap...  73.5 us
    unnamed x16, local copies, waits for them, and re-layouts  13.7 us
    pallas_call x1, Pallas kernels, on_device(): pl.pallas_call(functools.partial(attend_kernel, rows), grid_spec=pltpu.Pr...  10.9 us

profile of v1, /device:TPU:29, one launch (start us, length us, event | category | flops | bytes accessed | tf_op | source)
XLA Modules:
  0.0 100.4 jit_solution(5997209895293126632)
XLA Ops:
  0.0 0.7 and_select_fusion.1
  0.7 0.2 convert_reduce_fusion
  0.9 0.7 select_reduce_fusion.3
  1.6 0.1 sub.11
  1.7 0.1 stack_reshape.4
  1.8 0.9 copy.23
  2.8 0.0 copy-start.4
  2.9 1.1 %copy-done.4 = bf16[448,576]{1,0:T(8,128)(2,1)S(1)} copy-done((bf16[448,576]{1,0:T(8,128)(2,1)S(1)}, bf16[448,576]{1,0:T(8,128)(2,1)}, u32[]{:S(2)}) %copy-start.4) | copy-done | bytes 516120
  3.9 0.0 copy-start.5
  3.9 0.7 copy-done.5
  4.6 73.5 %shard_map.91 = (bf16[2,8,96,576]{3,2,1,0:T(8,128)(2,1)S(1)}, s32[8,8,128]{2,1,0:T(8,128)S(1)}, f32[32,576]{1,0:T(8,128)S(1)}) custom-call(s32[24]{0:T(128)S(1)} %get-tuple-element.17.send_prompt, bf16[12,64,3584]{2,1,0:T(8,128)(2,1)} %hidden.1, bf16[32,3584]{1,0:T(8,128)(2,1)S(1)} %pad.8.step_rows, bf16[448,576]{1,0:T(8,128)(2,1)S(1)} %copy-done.4, ...), custom_call_target="tpu_custom_call" | custom-call | tf_op jit(solution)/shard_map/pallas_call | solution.py:402
  78.1 0.0 copy-start.2
  78.1 1.3 %copy-done.2 = bf16[2,8,96,576]{3,2,1,0:T(8,128)(2,1)} copy-done((bf16[2,8,96,576]{3,2,1,0:T(8,128)(2,1)}, bf16[2,8,96,576]{3,2,1,0:T(8,128)(2,1)S(1)}, u32[]{:S(2)}) %copy-start.2) | copy-done | bytes 1769496
  79.4 0.1 broadcast_in_dim.61
  79.5 0.1 eq.49
  79.6 0.1 select_reduce_fusion
  79.7 0.0 copy-start.1
  79.7 0.0 copy-start.6
  79.7 6.1 %copy.26.cache = bf16[12,256,576]{2,1,0:T(8,128)(2,1)} copy(bf16[12,256,576]{1,2,0:T(8,128)(2,1)} %param.14) | data formatting | bytes 7077888 | tf_op args[5]
  85.8 0.0 copy-done.1
  85.8 0.0 copy-done.6
  85.8 2.1 %copy-done = bf16[12,256,576]{2,1,0:T(8,128)(2,1)S(1)} copy-done((bf16[12,256,576]{2,1,0:T(8,128)(2,1)S(1)}, bf16[12,256,576]{2,1,0:T(8,128)(2,1)}, u32[]{:S(2)}) %copy-start) | copy-done | bytes 3538968
  87.9 1.5 %copy-done.3 = bf16[2,8,96,576]{3,2,1,0:T(8,128)(2,1)S(1)} copy-done((bf16[2,8,96,576]{3,2,1,0:T(8,128)(2,1)S(1)}, bf16[2,8,96,576]{3,2,1,0:T(8,128)(2,1)}, u32[]{:S(2)}) %copy-start.3) | copy-done | bytes 1769496
  89.5 10.9 %shard_map.92 = bf16[2,12,64,512]{3,2,1,0:T(8,128)(2,1)} custom-call(s32[12]{0:T(128)S(1)} %get-tuple-element.14.slot_of, s32[12]{0:T(128)S(1)} %get-tuple-element.13.arrived_len, s32[12]{0:T(128)S(1)} %copy-done.6, bf16[2,12,64,576]{3,2,1,0:T(8,128)(2,1)S(1)} %copy-done.1, bf16[12,256,576]{2,1,0:T(8,128)(2,1)S(1)} %copy-done, ...), custom_call_target="tpu_custom_call" | custom-call | tf_op jit(solution)/shard_map/pallas_call | solution.py:457
  (9 shorter events, 0.1 us)
Async XLA Ops:
  2.8 1.1 %copy-start.4 = (bf16[448,576]{1,0:T(8,128)(2,1)S(1)}, bf16[448,576]{1,0:T(8,128)(2,1)}, u32[]{:S(2)}) copy-start(bf16[448,576]{1,0:T(8,128)(2,1)} %weight.1) | copy-start | bytes 1548292
  3.9 0.7 copy-start.5
  78.1 1.3 %copy-start.2 = (bf16[2,8,96,576]{3,2,1,0:T(8,128)(2,1)}, bf16[2,8,96,576]{3,2,1,0:T(8,128)(2,1)S(1)}, u32[]{:S(2)}) copy-start(bf16[2,8,96,576]{3,2,1,0:T(8,128)(2,1)S(1)} %get-tuple-element.9) | copy-start | bytes 5308420
  79.7 6.1 %copy-start.1 = (bf16[2,12,64,576]{3,2,1,0:T(8,128)(2,1)S(1)}, bf16[2,12,64,576]{3,2,1,0:T(8,128)(2,1)}, u32[]{:S(2)}) copy-start(bf16[2,12,64,576]{3,2,1,0:T(8,128)(2,1)} %query.1) | copy-start | bytes 5308420
  79.7 6.1 %copy-start.6 = (s32[12]{0:T(128)S(1)}, s32[12]{0:T(128)}, u32[]{:S(2)}) copy-start(s32[12]{0:T(128)} %cache_len.1) | copy-start | bytes 148
  85.8 2.1 %copy-start = (bf16[12,256,576]{2,1,0:T(8,128)(2,1)S(1)}, bf16[12,256,576]{2,1,0:T(8,128)(2,1)}, u32[]{:S(2)}) copy-start(bf16[12,256,576]{2,1,0:T(8,128)(2,1)} %copy.26.cache) | copy-start | bytes 10616836
  87.9 1.5 %copy-start.3 = (bf16[2,8,96,576]{3,2,1,0:T(8,128)(2,1)S(1)}, bf16[2,8,96,576]{3,2,1,0:T(8,128)(2,1)}, u32[]{:S(2)}) copy-start(bf16[2,8,96,576]{3,2,1,0:T(8,128)(2,1)} %copy-done.2) | copy-start | bytes 5308420

commit v2 on v1

v2 whole, which is shorter than its diff:
```python
import functools

import jax
import jax.numpy as jnp
from jax import lax
from jax.experimental import pallas as pl
from jax.experimental.pallas import tpu as pltpu
from jax.sharding import PartitionSpec as P

ROPE = 64
NOPE = 128
BLOCKS = 4
TILE = 16
MESH = pl.DeviceIdType.MESH


def ring_place(index, n, snake):
    if not snake:
        return index
    plane, column = lax.div(index, 2), lax.rem(index, 2)
    return plane + column * (n - 1 - 2 * plane)


def ring_index(place, n, snake):
    place = lax.rem(place + n, n)
    if not snake:
        return place
    back = lax.div(place, n // 2)
    return (1 - back) * 2 * place + back * (2 * (n - 1 - place) + 1)


def serve_kernel(
    n,
    cap,
    snake,
    prompt_dest,
    prompt_len,
    cache_len,
    hidden,
    step_rows,
    weight,
    gain,
    cache,
    queries,
    out,
    hbuf,
    wall,
    acc,
    other,
    pages,
    outbox,
    inbox,
    labels,
    meta,
    fresh,
    cached,
    asked,
    mixed,
    top,
    total,
    result,
    send_prompt,
    slot_of,
    arrived_len,
    local_sem,
    ring_send,
    ring_recv,
    cross_send,
    cross_recv,
    pair_send,
    pair_recv,
    page_send,
    page_recv,
    mate_send,
    mate_recv,
    meta_send,
    meta_recv,
    out_sem,
):
    rows, tokens, depth = hidden.shape
    half = tokens // 2
    shard, width = weight.shape
    latent_width = gain.shape[1]
    near = ((shard + TILE - 1) // (3 * TILE)) * TILE
    far = shard - near
    steps = n // 2

    group = lax.axis_index("groups")
    me = lax.axis_index("seq")
    core = lax.axis_index("head")
    side = lax.rem(group, 2)
    twin = {"groups": group + 1 - 2 * side, "seq": me, "head": core}
    mate = {"groups": group, "seq": me, "head": 1 - core}

    def peer(index):
        return {"groups": group, "seq": index, "head": core}

    place = ring_place(me, n, snake)

    own = pltpu.make_async_copy(weight, wall.at[me], local_sem.at[0])
    own.start()
    loads = [
        pltpu.make_async_copy(
            hidden.at[:, pl.ds(pl.multiple_of((1 - core) * half, half), half), :],
            hbuf.at[pl.ds(0, rows)],
            local_sem.at[1],
        ),
        pltpu.make_async_copy(step_rows, hbuf.at[rows], local_sem.at[2]),
        pltpu.make_async_copy(
            hidden.at[:, pl.ds(pl.multiple_of(core * half, half), half), :],
            hbuf.at[pl.ds(rows + 1, rows)],
            local_sem.at[3],
        ),
    ]
    late_loads = [
        pltpu.make_async_copy(cache, cached, local_sem.at[4]),
        pltpu.make_async_copy(queries, asked, local_sem.at[5]),
    ]

    barrier = pltpu.get_barrier_semaphore()
    for offset in range(1, n):
        pl.semaphore_signal(
            barrier, inc=1, device_id=peer(lax.rem(me + offset, n)), device_id_type=MESH
        )
    pl.semaphore_signal(barrier, inc=1, device_id=twin, device_id_type=MESH)
    pl.semaphore_signal(barrier, inc=1, device_id=mate, device_id_type=MESH)
    pl.semaphore_wait(barrier, n + 1)
    own.wait()

    def span(chunk, which):
        if chunk == 0:
            return pl.ds(pl.multiple_of(which * far, TILE), near)
        return pl.ds(near, far - near)

    def ring_copy(way, step, chunk):
        sign = 1 - 2 * way
        block = wall.at[ring_index(place - sign * (step - 1), n, snake), span(chunk, side)]
        return pltpu.make_async_remote_copy(
            src_ref=block,
            dst_ref=block,
            send_sem=ring_send.at[way, step - 1, chunk],
            recv_sem=ring_recv.at[way, step - 1, chunk],
            device_id=peer(ring_index(place + sign, n, snake)),
            device_id_type=MESH,
        )

    def ring_arrival(way, step, chunk):
        sign = 1 - 2 * way
        block = wall.at[ring_index(place - sign * step, n, snake), span(chunk, side)]
        return pltpu.make_async_remote_copy(
            src_ref=block,
            dst_ref=block,
            send_sem=ring_send.at[way, step - 1, chunk],
            recv_sem=ring_recv.at[way, step - 1, chunk],
            device_id=peer(ring_index(place + sign, n, snake)),
            device_id_type=MESH,
        )

    def cross_copy(way, step, which):
        sign = 1 - 2 * way
        block = wall.at[ring_index(place - sign * step, n, snake), span(0, which)]
        return pltpu.make_async_remote_copy(
            src_ref=block,
            dst_ref=block,
            send_sem=cross_send.at[way, step - 1],
            recv_sem=cross_recv.at[way, step - 1],
            device_id=twin,
            device_id_type=MESH,
        )

    def goes(way, step, chunk):
        return step < steps or (step == steps and way == chunk)

    for chunk in (0, 1):
        for way in (0, 1):
            if goes(way, 1, chunk):
                ring_copy(way, 1, chunk).start()
    for load in loads:
        load.start()

    for load in late_loads:
        load.start()

    def meta_copy(target, row):
        return pltpu.make_async_remote_copy(
            src_ref=labels,
            dst_ref=meta.at[row],
            send_sem=meta_send.at[target],
            recv_sem=meta_recv.at[row],
            device_id=peer(target),
            device_id_type=MESH,
        )

    lane = lax.broadcasted_iota(jnp.int32, (1, 128), 1)
    dest = jnp.full((1, 128), -1, jnp.int32)
    live = jnp.zeros((1, 128), jnp.int32)
    order = jnp.zeros((1, 128), jnp.int32)
    for prompt in range(rows):
        dest = jnp.where(lane == prompt, prompt_dest[prompt], dest)
        live = jnp.where(lane == prompt, prompt_len[prompt], live)
    owner = jnp.full((1, 128), -1, jnp.int32)
    for prompt in range(rows):
        one = lax.div(prompt_dest[prompt], rows)
        owner = jnp.where(lane == prompt, one, owner)
    for prompt in range(rows):
        one = lax.div(prompt_dest[prompt], rows)
        order = order + jnp.where((lane > prompt) & (owner == one), 1, 0)
    labels[...] = jnp.zeros(labels.shape, jnp.int32)
    labels[0:1, :] = dest
    labels[1:2, :] = live
    labels[2:3, :] = order
    for offset in range(1, n):
        meta_copy(lax.rem(me + offset, n), me).start()
    meta[me] = labels[...]
    place_sent = owner * cap + order

    def find_prompt(slot, carry):
        send_prompt[slot] = jnp.minimum(
            jnp.sum(jnp.where(place_sent == slot, lane, 0)), rows - 1
        )
        return carry

    lax.fori_loop(0, n * cap, find_prompt, 0)
    for load in loads:
        load.wait()

    depth_block = depth // BLOCKS
    shards_block = n // BLOCKS
    lower = pl.ds(0, rows + 1)
    upper = pl.ds(rows + 1, rows)

    def block_at(turn):
        if not snake:
            return jnp.int32(turn)
        plane = lax.div(me, 2)
        late = lax.div(plane, BLOCKS // 2)
        edge = plane + late * (BLOCKS - 1 - 2 * plane)
        base = (jnp.int32(0), jnp.int32(1), 2 + edge, 3 - edge)[turn]
        return base + late * (BLOCKS - 1 - 2 * base)

    def multiply(turn, part, count):
        block = block_at(turn)
        columns = pl.ds(pl.multiple_of(block * depth_block, 128), depth_block)
        left = hbuf[part, :, columns].reshape(count * half, depth_block)
        right = wall[pl.ds(block * shards_block, shards_block)].reshape(depth_block, width)
        product = jnp.dot(left, right, preferred_element_type=jnp.float32)
        product = product.reshape(count, half, width)
        if turn == 0:
            acc[part] = product
        else:
            acc[part] += product

    if snake:
        ready = {(2, 1): (0,), (3, 1): (1,), (4, 0): (2,), (4, 1): (3,)}
    else:
        ready = {(steps, 1): tuple(range(BLOCKS))}
    crossed = []
    for step in range(1, steps + 1):
        for chunk in (0, 1):
            for way in (0, 1):
                if not goes(way, step, chunk):
                    continue
                ring_arrival(way, step, chunk).wait_recv()
                if step < steps and goes(way, step + 1, chunk):
                    ring_copy(way, step + 1, chunk).start()
                if chunk == 0:
                    cross_copy(way, step, side).start()
                    crossed.append((way, step))
            turns = ready.get((step, chunk), ())
            if turns:
                waiting = [pair for pair in crossed if chunk == 1 or pair[1] < step]
                for way, when in waiting:
                    cross_copy(way, when, 1 - side).wait_recv()
                crossed = [pair for pair in crossed if pair not in waiting]
            for turn in turns:
                multiply(turn, lower, rows + 1)
                if turn == BLOCKS - 1:
                    pair = pltpu.make_async_remote_copy(
                        src_ref=acc.at[lower],
                        dst_ref=other,
                        send_sem=pair_send,
                        recv_sem=pair_recv,
                        device_id=mate,
                        device_id_type=MESH,
                    )
                    pair.start()
                multiply(turn, upper, rows)
    pair.wait()

    scale = gain[...]

    def norm(value):
        latent = value[:, :latent_width]
        mean_square = jnp.mean(latent * latent, axis=-1, keepdims=True)
        return latent * lax.rsqrt(mean_square + 1e-06) * scale, value[:, latent_width:]

    def norm_page(row, carry):
        value = acc[rows + 1 + row] + other[row]
        head_part, tail_part = norm(value)
        pages[row, :, :latent_width] = head_part.astype(jnp.bfloat16)
        pages[row, :, latent_width:] = tail_part.astype(jnp.bfloat16)
        return carry

    lax.fori_loop(0, rows, norm_page, 0)

    def page_copy(target, row):
        return pltpu.make_async_remote_copy(
            src_ref=outbox.at[target],
            dst_ref=inbox.at[core, pl.ds(row * cap, cap)],
            send_sem=page_send.at[target],
            recv_sem=page_recv.at[row],
            device_id=peer(target),
            device_id_type=MESH,
        )

    def mate_copy(row, where):
        block = inbox.at[where, pl.ds(row * cap, cap)]
        return pltpu.make_async_remote_copy(
            src_ref=block,
            dst_ref=block,
            send_sem=mate_send.at[row],
            recv_sem=mate_recv.at[row],
            device_id=mate,
            device_id_type=MESH,
        )

    for offset in range(1, n):
        target = lax.rem(me + offset, n)
        for slot in range(cap):
            outbox[target, slot] = pages[send_prompt[target * cap + slot]]
        page_copy(target, me).start()
    for slot in range(cap):
        inbox[core, me * cap + slot] = pages[send_prompt[me * cap + slot]]
    mate_copy(me, core).start()

    head_part, tail_part = norm(acc[rows] + other[rows])
    fresh[:, :latent_width] = head_part.astype(jnp.bfloat16).astype(jnp.float32)
    fresh[:, latent_width:] = tail_part.astype(jnp.bfloat16).astype(jnp.float32)

    for step in range(1, steps + 1):
        for chunk in (0, 1):
            for way in (0, 1):
                if goes(way, step, chunk):
                    ring_copy(way, step, chunk).wait_send()
                    if chunk == 0:
                        cross_copy(way, step, side).wait_send()
    for offset in range(1, n):
        target = lax.rem(me + offset, n)
        meta_copy(target, me).wait_send()
        meta_copy(target, target).wait_recv()
    came = meta[:, 0, :]
    came_len = meta[:, 1, :]
    came_slot = lax.broadcasted_iota(jnp.int32, came.shape, 0) * cap + meta[:, 2, :]

    def find_slot(row, carry):
        here = came == me * rows + row
        slot_of[row] = jnp.minimum(jnp.sum(jnp.where(here, came_slot, 0)), n * cap - 1)
        arrived_len[row] = jnp.sum(jnp.where(here, came_len, 0))
        return carry

    lax.fori_loop(0, rows, find_slot, 0)
    for load in late_loads:
        load.wait()

    step_count, _, heads, _ = queries.shape
    asking = step_count * heads
    score_scale = (NOPE + ROPE) ** (-0.5)
    contract = (((1,), (1,)), ((), ()))

    def against(left, right):
        return lax.dot_general(left, right, contract, preferred_element_type=jnp.float32)

    def attend_resident(row, carry):
        spot = lax.broadcasted_iota(jnp.int32, (TILE, width), 0)
        tail = jnp.zeros((TILE, width), jnp.float32)
        for step in range(step_count):
            tail = jnp.where(spot == step, fresh[pl.ds(step * rows + row, 1), :], tail)
        tail = tail.astype(jnp.bfloat16)
        query = asked[:, row].reshape(asking, width)
        old = jnp.dot(query, cached[row], preferred_element_type=jnp.float32)
        new = against(query, tail)
        old_spot = lax.broadcasted_iota(jnp.int32, old.shape, 1)
        new_spot = lax.broadcasted_iota(jnp.int32, new.shape, 1)
        step_of = lax.div(lax.broadcasted_iota(jnp.int32, new.shape, 0), heads)
        old = jnp.where(old_spot < cache_len[row], old * score_scale, -jnp.inf)
        new = jnp.where(new_spot <= step_of, new * score_scale, -jnp.inf)
        peak = jnp.maximum(
            jnp.max(old, axis=-1, keepdims=True), jnp.max(new, axis=-1, keepdims=True)
        )
        old = jnp.exp(old - peak)
        new = jnp.exp(new - peak)
        top[row] = peak
        total[row] = jnp.sum(old, axis=-1, keepdims=True) + jnp.sum(
            new, axis=-1, keepdims=True
        )
        mixed[row] = against(
            old.astype(jnp.bfloat16), cached[row, pl.ds(0, latent_width), :]
        ) + jnp.dot(
            new.astype(jnp.bfloat16),
            tail[:, :latent_width],
            preferred_element_type=jnp.float32,
        )
        return carry

    done = 0
    for offset in range(1, n):
        until = rows * offset // (n - 1)
        if until > done:
            lax.fori_loop(done, until, attend_resident, 0)
            done = until
        source = lax.rem(me + n - offset, n)
        page_copy(source, source).wait_recv()
        mate_copy(source, core).start()
    for offset in range(1, n):
        page_copy(lax.rem(me + offset, n), me).wait_send()
    for offset in range(n):
        source = lax.rem(me + n - offset, n)
        mate_copy(source, 1 - core).wait_recv()
        mate_copy(source, core).wait_send()

    def out_copy(row):
        return pltpu.make_async_copy(result.at[row], out.at[:, row], out_sem.at[row])

    def attend_prompt(row, carry):
        keys = inbox[:, slot_of[row]].reshape(tokens, width)
        query = asked[:, row].reshape(asking, width)
        score = against(query, keys)
        spot = lax.broadcasted_iota(jnp.int32, score.shape, 1)
        score = jnp.where(spot < arrived_len[row], score * score_scale, -jnp.inf)
        before = top[row]
        peak = jnp.maximum(before, jnp.max(score, axis=-1, keepdims=True))
        fade = jnp.exp(before - peak)
        part = jnp.exp(score - peak)
        inverse = 1.0 / (total[row] * fade + jnp.sum(part, axis=-1, keepdims=True))
        value = mixed[row] * (fade * inverse) + inverse * jnp.dot(
            part.astype(jnp.bfloat16),
            keys[:, :latent_width],
            preferred_element_type=jnp.float32,
        )
        result[row] = value.astype(jnp.bfloat16).reshape(step_count, heads, latent_width)
        out_copy(row).start()
        return carry

    lax.fori_loop(0, rows, attend_prompt, 0, unroll=2)
    for row in range(rows):
        out_copy(row).wait()


def on_device(
    snake,
    prompt_hidden,
    prompt_len,
    prompt_dest,
    kv_weight,
    kv_gain,
    cache,
    cache_len,
    step_hidden,
    queries,
):
    rows, tokens, depth = prompt_hidden.shape
    step_count = step_hidden.shape[0]
    shard, width = kv_weight.shape
    resident_slots = cache.shape[1]
    latent_width = kv_gain.shape[0]
    heads = queries.shape[2]
    n = lax.axis_size("seq")
    cap = max(1, 2 * rows // n)
    half = tokens // 2

    step_rows = step_hidden.reshape(step_count * rows, depth)
    step_rows = jnp.pad(step_rows, ((0, half - step_count * rows), (0, 0)))

    dma = pltpu.SemaphoreType.DMA
    anywhere = pl.BlockSpec(memory_space=pl.ANY)
    scalars = pl.BlockSpec(memory_space=pltpu.SMEM)
    asking = step_count * heads
    return pl.pallas_call(
        functools.partial(serve_kernel, n, cap, snake),
        out_shape=jax.ShapeDtypeStruct((step_count, rows, heads, latent_width), jnp.bfloat16),
        in_specs=[scalars] * 3
        + [anywhere] * 3
        + [pl.BlockSpec(memory_space=pltpu.VMEM)]
        + [anywhere] * 2,
        out_specs=anywhere,
        scratch_shapes=[
            pltpu.VMEM((2 * rows + 1, half, depth), jnp.bfloat16),
            pltpu.VMEM((n, shard, width), jnp.bfloat16),
            pltpu.VMEM((2 * rows + 1, half, width), jnp.float32),
            pltpu.VMEM((rows + 1, half, width), jnp.float32),
            pltpu.VMEM((rows, half, width), jnp.bfloat16),
            pltpu.VMEM((n, cap, half, width), jnp.bfloat16),
            pltpu.VMEM((2, n * cap, half, width), jnp.bfloat16),
            pltpu.VMEM((8, 128), jnp.int32),
            pltpu.VMEM((n, 8, 128), jnp.int32),
            pltpu.VMEM((half, width), jnp.float32),
            pltpu.VMEM((rows, width, resident_slots), jnp.bfloat16),
            pltpu.VMEM(queries.shape, jnp.bfloat16),
            pltpu.VMEM((rows, asking, latent_width), jnp.float32),
            pltpu.VMEM((rows, asking, 1), jnp.float32),
            pltpu.VMEM((rows, asking, 1), jnp.float32),
            pltpu.VMEM((rows, step_count, heads, latent_width), jnp.bfloat16),
            pltpu.SMEM((n * cap,), jnp.int32),
            pltpu.SMEM((rows,), jnp.int32),
            pltpu.SMEM((rows,), jnp.int32),
            dma((6,)),
            dma((2, n // 2, 2)),
            dma((2, n // 2, 2)),
            dma((2, n // 2)),
            dma((2, n // 2)),
            dma,
            dma,
            dma((n,)),
            dma((n,)),
            dma((n,)),
            dma((n,)),
            dma((n,)),
            dma((n,)),
            dma((rows,)),
        ],
        compiler_params=pltpu.CompilerParams(
            collective_id=0, has_side_effects=True, vmem_limit_bytes=60 * 1024 * 1024
        ),
    )(
        prompt_dest,
        prompt_len,
        cache_len,
        prompt_hidden,
        step_rows,
        kv_weight,
        kv_gain.reshape(1, latent_width),
        jnp.transpose(cache, (0, 2, 1)),
        queries,
    )


def solution(mesh):
    snake = mesh.shape["seq"] == 2 * BLOCKS
    in_specs = (
        P(("groups", "seq"), None, "head"),
        P(("groups", "seq")),
        P(("groups", "seq")),
        P(("head", "seq"), None),
        P(),
        P(("groups", "seq"), None, None),
        P(("groups", "seq")),
        P(None, ("groups", "seq"), "head"),
        P(None, ("groups", "seq"), "head", None),
    )
    out_specs = P(None, ("groups", "seq"), "head", None)
    return jax.shard_map(
        functools.partial(on_device, snake),
        mesh=mesh,
        in_specs=in_specs,
        out_specs=out_specs,
        check_vma=False,
    )
```

time: 101 us -> 84.8 us (0.84)
  local copies, waits for them, and re-layouts: 14.1 us -> 4.4 us
  Pallas kernels: 84.4 us -> 80.2 us
  other arithmetic: 1.74 us -> 0 us
    unnamed x16 -> x2, local copies, waits for them, and re-layouts: 13.7 us -> 3.65 us
    pallas_call x2 -> x1, Pallas kernels: 84.4 us -> 80.2 us  [on_device(): pl.pallas_call(functools.partial(serve_kernel, n, cap, snake), out_shape=...]
    reduce_sum x3 -> x0, other arithmetic: 1.05 us -> none  [the longest x1 0.74 us: on_device(): jnp.sum(jnp.where(fits, prompt_dest[None, :] % rows + 1, 0), axis=1) - 1]
where the time goes in v2:
time: 84.8 us; the launch traced here: 84.6 us
  Pallas kernels  80.2 us (95%)
  local copies, waits for them, and re-layouts  4.4 us (5%)
    pallas_call x1, Pallas kernels, on_device(): pl.pallas_call(functools.partial(serve_kernel, n, cap, snake), out_shape=...  80.2 us
    unnamed x2, local copies, waits for them, and re-layouts  3.65 us

profile of v2, /device:TPU:29, one launch (start us, length us, event | category | flops | bytes accessed | tf_op | source)
XLA Modules:
  0.0 84.6 jit_solution(1473499256582449368)
XLA Ops:
  0.0 0.9 %copy.11 = bf16[2,12,3584]{2,1,0:T(8,128)(2,1)S(1)} copy(bf16[2,12,3584]{2,0,1:T(2,128)(2,1)} %param.16) | data formatting | bytes 344064 | tf_op args[7]
  1.0 0.7 pad.4.step_rows
  1.7 80.2 %shard_map.91 = bf16[2,12,64,512]{3,2,1,0:T(8,128)(2,1)} custom-call(s32[12]{0:T(128)} %prompt_dest.1, s32[12]{0:T(128)} %prompt_len.1, s32[12]{0:T(128)} %cache_len.1, bf16[12,64,3584]{2,1,0:T(8,128)(2,1)} %hidden.1, bf16[32,3584]{1,0:T(8,128)(2,1)} %pad.4.step_rows, bf16[448,576]{1,0:T(8,128)(2,1)} %weight.1, f32[1,512]{1,0:T(1,128)} %bitcast.3, ...), custom_call_target="tpu_custom_call" | custom-call | tf_op jit(solution)/shard_map/pallas_call | solution.py:478
  81.9 2.7 %copy.13 = bf16[2,12,64,512]{3,2,1,0:T(8,128)(2,1)} copy(bf16[2,12,64,512]{3,2,1,0:T(8,128)(2,1)} %shard_map.91) | data formatting | bytes 3145728
  (1 shorter events, 0.0 us)

commit v3 on v2

--- a/solution.py
+++ b/solution.py
@@ -46,6 +46,7 @@
     hbuf,
     wall,
     acc,
+    sent,
     other,
     pages,
     outbox,
@@ -105,7 +106,6 @@
             hbuf.at[pl.ds(0, rows)],
             local_sem.at[1],
         ),
-        pltpu.make_async_copy(step_rows, hbuf.at[rows], local_sem.at[2]),
         pltpu.make_async_copy(
             hidden.at[:, pl.ds(pl.multiple_of(core * half, half), half), :],
             hbuf.at[pl.ds(rows + 1, rows)],
@@ -177,6 +177,8 @@
                 ring_copy(way, 1, chunk).start()
     for load in loads:
         load.start()
+    spare = jnp.zeros((half - step_rows.shape[0], depth), jnp.bfloat16)
+    hbuf[rows] = jnp.concatenate([step_rows[...], spare], axis=0)
 
     for load in late_loads:
         load.start()
@@ -220,7 +222,7 @@
         )
         return carry
 
-    lax.fori_loop(0, n * cap, find_prompt, 0)
+    lax.fori_loop(0, n * cap, find_prompt, 0, unroll=8)
     for load in loads:
         load.wait()
 
@@ -247,6 +249,10 @@
         product = product.reshape(count, half, width)
         if turn == 0:
             acc[part] = product
+        elif turn == BLOCKS - 1 and count > rows:
+            whole = acc[part] + product
+            sent[...] = whole.astype(jnp.bfloat16)
+            acc[rows] = whole[rows]
         else:
             acc[part] += product
 
@@ -276,7 +282,7 @@
                 multiply(turn, lower, rows + 1)
                 if turn == BLOCKS - 1:
                     pair = pltpu.make_async_remote_copy(
-                        src_ref=acc.at[lower],
+                        src_ref=sent,
                         dst_ref=other,
                         send_sem=pair_send,
                         recv_sem=pair_recv,
@@ -295,13 +301,13 @@
         return latent * lax.rsqrt(mean_square + 1e-06) * scale, value[:, latent_width:]
 
     def norm_page(row, carry):
-        value = acc[rows + 1 + row] + other[row]
+        value = acc[rows + 1 + row] + other[row].astype(jnp.float32)
         head_part, tail_part = norm(value)
         pages[row, :, :latent_width] = head_part.astype(jnp.bfloat16)
         pages[row, :, latent_width:] = tail_part.astype(jnp.bfloat16)
         return carry
 
-    lax.fori_loop(0, rows, norm_page, 0)
+    lax.fori_loop(0, rows, norm_page, 0, unroll=2)
 
     def page_copy(target, row):
         return pltpu.make_async_remote_copy(
@@ -333,7 +339,7 @@
         inbox[core, me * cap + slot] = pages[send_prompt[me * cap + slot]]
     mate_copy(me, core).start()
 
-    head_part, tail_part = norm(acc[rows] + other[rows])
+    head_part, tail_part = norm(acc[rows] + other[rows].astype(jnp.float32))
     fresh[:, :latent_width] = head_part.astype(jnp.bfloat16).astype(jnp.float32)
     fresh[:, latent_width:] = tail_part.astype(jnp.bfloat16).astype(jnp.float32)
 
@@ -358,7 +364,7 @@
         arrived_len[row] = jnp.sum(jnp.where(here, came_len, 0))
         return carry
 
-    lax.fori_loop(0, rows, find_slot, 0)
+    lax.fori_loop(0, rows, find_slot, 0, unroll=6)
     for load in late_loads:
         load.wait()
 
@@ -441,7 +447,7 @@
         out_copy(row).start()
         return carry
 
-    lax.fori_loop(0, rows, attend_prompt, 0, unroll=2)
+    lax.fori_loop(0, rows, attend_prompt, 0, unroll=4)
     for row in range(rows):
         out_copy(row).wait()
 
@@ -469,25 +475,25 @@
     half = tokens // 2
 
     step_rows = step_hidden.reshape(step_count * rows, depth)
-    step_rows = jnp.pad(step_rows, ((0, half - step_count * rows), (0, 0)))
 
     dma = pltpu.SemaphoreType.DMA
     anywhere = pl.BlockSpec(memory_space=pl.ANY)
+    in_hbm = pl.BlockSpec(memory_space=pltpu.HBM)
+    in_vmem = pl.BlockSpec(memory_space=pltpu.VMEM)
     scalars = pl.BlockSpec(memory_space=pltpu.SMEM)
     asking = step_count * heads
     return pl.pallas_call(
         functools.partial(serve_kernel, n, cap, snake),
         out_shape=jax.ShapeDtypeStruct((step_count, rows, heads, latent_width), jnp.bfloat16),
         in_specs=[scalars] * 3
-        + [anywhere] * 3
-        + [pl.BlockSpec(memory_space=pltpu.VMEM)]
-        + [anywhere] * 2,
+        + [in_hbm, in_vmem, in_hbm, in_vmem, in_hbm, in_hbm],
         out_specs=anywhere,
         scratch_shapes=[
             pltpu.VMEM((2 * rows + 1, half, depth), jnp.bfloat16),
             pltpu.VMEM((n, shard, width), jnp.bfloat16),
             pltpu.VMEM((2 * rows + 1, half, width), jnp.float32),
-            pltpu.VMEM((rows + 1, half, width), jnp.float32),
+            pltpu.VMEM((rows + 1, half, width), jnp.bfloat16),
+            pltpu.VMEM((rows + 1, half, width), jnp.bfloat16),
             pltpu.VMEM((rows, half, width), jnp.bfloat16),
             pltpu.VMEM((n, cap, half, width), jnp.bfloat16),
             pltpu.VMEM((2, n * cap, half, width), jnp.bfloat16),
@@ -519,7 +525,7 @@
             dma((rows,)),
         ],
         compiler_params=pltpu.CompilerParams(
-            collective_id=0, has_side_effects=True, vmem_limit_bytes=60 * 1024 * 1024
+            collective_id=0, has_side_effects=True, vmem_limit_bytes=60300 * 1024
         ),
     )(
         prompt_dest,

time: 84.8 us -> 83.3 us (0.982)
  Pallas kernels: 80.2 us -> 78.8 us
    pallas_call x1, Pallas kernels: 80.2 us -> 78.8 us  [on_device(): pl.pallas_call(functools.partial(serve_kernel, n, cap, snake), out_shape=...]
where the time goes in v3:
time: 83.3 us; the launch traced here: 83.1 us
  Pallas kernels  78.8 us (95%)
  local copies, waits for them, and re-layouts  4.36 us (5%)
    pallas_call x1, Pallas kernels, on_device(): pl.pallas_call(functools.partial(serve_kernel, n, cap, snake), out_shape=...  78.8 us
    unnamed x2, local copies, waits for them, and re-layouts  3.65 us

profile of v3, /device:TPU:29, one launch (start us, length us, event | category | flops | bytes accessed | tf_op | source)
XLA Modules:
  0.0 83.1 jit_solution(8521442731102015238)
XLA Ops:
  0.0 0.9 %copy.11 = bf16[2,12,3584]{2,1,0:T(8,128)(2,1)S(1)} copy(bf16[2,12,3584]{2,0,1:T(2,128)(2,1)} %param.16) | data formatting | bytes 344064 | tf_op args[7]
  0.9 0.7 reshape.6.step_rows
  1.7 78.8 %shard_map.91 = bf16[2,12,64,512]{3,2,1,0:T(8,128)(2,1)} custom-call(s32[12]{0:T(128)} %prompt_dest.1, s32[12]{0:T(128)} %prompt_len.1, s32[12]{0:T(128)} %cache_len.1, bf16[12,64,3584]{2,1,0:T(8,128)(2,1)} %hidden.1, bf16[24,3584]{1,0:T(8,128)(2,1)} %reshape.6.step_rows, bf16[448,576]{1,0:T(8,128)(2,1)} %weight.1, f32[1,512]{1,0:T(1,128)} %bitcast.3, ...), custom_call_target="tpu_custom_call" | custom-call | tf_op jit(solution)/shard_map/pallas_call | solution.py:485
  80.4 2.7 %copy.13 = bf16[2,12,64,512]{3,2,1,0:T(8,128)(2,1)} copy(bf16[2,12,64,512]{3,2,1,0:T(8,128)(2,1)} %shard_map.91) | data formatting | bytes 3145728
